TPU v7x, 512 devices: a whole 4x8x8 slice. The times are simulated.
512 devices in a mesh: row: 16 (over y, z_hi), col: 32 (over z_lo, x, core).
Axes of the slice: x: 4, y: 8, z: 8 (z_hi: 2, z_lo: 4; z = z_hi * 4 + z_lo), core: 2. Of those that a mesh axis runs over, the one named last changes fastest.
Arguments:
- question_vectors: float32 [2048, 4096], P('row', 'col'), may hold values from -1 to 1
- document_vectors: float32 [8192, 4096], P('col', 'row'), may hold values from -1 to 1
- positive: int32 [2048], P('row'), may hold values from 0 to 3
Outputs:
- loss_value: float32 [], replicated
- question_vector_derivative: float32 [2048, 4096], P('row', 'col')
- document_vector_derivative: float32 [8192, 4096], P('col', 'row')
All inputs are finite; a program needn't handle non-finite values.
Results may differ from a plain program's by a relative error of at most 0.00065.
Values sent between devices are 32-bit elements; how exact they have to be, the bound alone decides.
A program may use at most 64 MiB of HBM per device.

v0:
```python
import jax
import jax.numpy as jnp
from jax import lax
from jax.sharding import PartitionSpec as P

LIST = 4


sharpness_divisor = 0.05


def body(question_vectors, document_vectors, positive):
    biggest_match_level = lax.Precision.HIGHEST
    query_count = question_vectors.shape[0]
    full_queries = lax.all_gather(question_vectors, "col", axis=1, tiled=True)
    gathered_passage_rows = lax.all_gather(document_vectors, "row", axis=1, tiled=True)
    passage_count = gathered_passage_rows.shape[0]
    match_raw_levels = (
        jnp.dot(
            full_queries,
            gathered_passage_rows.T,
            precision=biggest_match_level,
            preferred_element_type=jnp.float32,
        )
        / sharpness_divisor
    )
    first_query = lax.axis_index("row") * query_count
    first_passage = lax.axis_index("col") * passage_count
    target_index = LIST * (first_query + jnp.arange(query_count, dtype=jnp.int32)) + positive
    local_index = first_passage + jnp.arange(passage_count, dtype=jnp.int32)
    positive_hit = (target_index[:, None] == local_index[None, :]).astype(jnp.float32)
    positive_local = jnp.sum(match_raw_levels * positive_hit, axis=1)
    local_top = jnp.max(match_raw_levels, axis=1)
    topmost = lax.pmax(local_top, "col")
    local_total = jnp.sum(jnp.exp(match_raw_levels - topmost[:, None]), axis=1)
    exp_total, positive_score = lax.psum((local_total, positive_local), "col")
    log_total = topmost + jnp.log(exp_total)
    query_score_sum = query_count * lax.axis_size("row")
    loss_value = lax.psum(jnp.sum(log_total - positive_score), "row") / query_score_sum
    normalized_likelihoods = jnp.exp(match_raw_levels - log_total[:, None]) - positive_hit
    query_terms = (
        jnp.dot(
            normalized_likelihoods,
            gathered_passage_rows,
            precision=biggest_match_level,
            preferred_element_type=jnp.float32,
        )
        / sharpness_divisor
    )
    question_vector_derivative = lax.psum_scatter(
        query_terms, "col", scatter_dimension=1, tiled=True
    )
    query_slices = lax.all_to_all(full_queries, "row", split_axis=1, concat_axis=0, tiled=True)
    weight_block = lax.all_gather(normalized_likelihoods, "row", axis=0, tiled=True)
    document_vector_derivative = (
        jnp.dot(
            weight_block.T,
            query_slices,
            precision=biggest_match_level,
            preferred_element_type=jnp.float32,
        )
        / sharpness_divisor
    )
    return (loss_value, question_vector_derivative, document_vector_derivative)


def solution(mesh):
    in_specs = (P("row", "col"), P("col", "row"), P("row"))
    out_specs = (P(), P("row", "col"), P("col", "row"))
    return jax.shard_map(body, mesh=mesh, in_specs=in_specs, out_specs=out_specs, check_vma=False)
```

profile of v0, /device:TPU:48, one launch (start us, length us, event | category | flops | bytes accessed | tf_op | source)
XLA Modules:
  0.0 658.3 jit_solution(14746167251565867420)
XLA Ops:
  7.2 0.0 all-gather.4.cloned.1.call-start
  7.2 1.6 copy.6
  8.8 0.0 all-gather.6.cloned.1.call-start
  8.9 0.7 all-gather.6.cloned.1.call-update
  9.6 0.0 all-gather.8.cloned.1.call-start
  9.6 0.7 multiply_add_fusion
  10.3 67.8 %all-gather.4.cloned.1.call-done = f32[128,4096]{0,1:T(8,128)} async-done(((f32[128,128]{0,1:T(8,128)}), f32[128,4096]{0,1:T(8,128)}) %all-gather.4.cloned.1.call-update) | async-done | bytes 2097168 | tf_op jit(solution)/shard_map/all_gather | solution.py:15
  78.1 141.5 %all-gather.6.cloned.1.call-done = f32[256,4096]{1,0:T(8,128)} async-done(((f32[256,256]{1,0:T(8,128)}), f32[256,4096]{1,0:T(8,128)}) %all-gather.6.cloned.1.call-update) | async-done | bytes 4194320 | tf_op jit(solution)/shard_map/all_gather | solution.py:16
  219.6 6.4 fusion.2
  226.0 67.4 %pmax.7 = f32[128]{0:T(128)S(1)} all-reduce(f32[128]{0:T(128)S(1)} %get-tuple-element.9), channel_id=1, replica_groups=mesh['row'=16,'col'=32] {'col'}, use_global_device_ids=true, to_apply=%region_1.0 | all-reduce | flops 128 | bytes 1024 | tf_op jit(solution)/shard_map/pmax | solution.py:34
  293.4 0.2 fusion
  293.6 67.7 %all-reduce = (f32[128]{0:T(128)S(1)}, f32[128]{0:T(128)S(1)}) all-reduce(f32[128]{0:T(128)S(1)} %get-tuple-element.4, f32[128]{0:T(128)S(1)} %get-tuple-element.3), channel_id=1, replica_groups=mesh['row'=16,'col'=32] {'col'}, use_global_device_ids=true, to_apply=%region_3.0 | all-reduce | flops 256 | bytes 2048 | tf_op jit(solution)/shard_map/psum | solution.py:36
  361.3 0.6 subtract_reduce_fusion
  361.9 0.8 fusion.1
  362.7 0.0 all-gather.8.cloned.1.call-update
  362.7 5.6 all-to-all-start
  368.3 0.0 reduce-scatter.2.cloned.1.call-start
  368.3 5.9 convolution_multiply_fusion
  374.2 0.0 reduce-scatter.2.cloned.1.call-update
  374.2 86.1 %psum.23 = f32[]{:T(128)} all-reduce(f32[]{:T(128)} %get-tuple-element.7), channel_id=1, replica_groups=mesh['row'=16,'col'=32] {'row'}, use_global_device_ids=true, to_apply=%region_7.0 | all-reduce | flops 1 | bytes 8 | tf_op jit(solution)/shard_map/psum | solution.py:39
  461.0 1.8 copy.7
  462.8 40.3 %all-gather.8.cloned.1.call-done = f32[2048,256]{1,0:T(8,128)} async-done(((f32[128,256]{1,0:T(8,128)}), f32[2048,256]{1,0:T(8,128)}) %all-gather.8.cloned.1.call-update) | async-done | bytes 2097168 | tf_op jit(solution)/shard_map/all_gather | solution.py:54
  503.1 6.4 convolution_multiply_fusion.1
  509.5 141.1 %reduce-scatter.2.cloned.1.call-done = f32[128,128]{1,0:T(8,128)} async-done(((f32[128,4096]{1,0:T(8,128)}), f32[128,128]{1,0:T(8,128)}) %reduce-scatter.2.cloned.1.call-update) | async-done | bytes 65552 | tf_op jit(solution)/shard_map/reduce_scatter | solution.py:50
  (5 shorter events, 0.0 us)
Async XLA Ops:
  7.2 70.9 %all-gather.4.cloned.1.call-start = ((), (), s32[]{:S(2)}) async-start(), calls=%async_computation.2 | async-start | bytes 2162688 | tf_op jit(solution)/shard_map/all_gather | solution.py:15
  8.8 210.8 %all-gather.6.cloned.1.call-start = ((), (), s32[]{:S(2)}) async-start(), calls=%async_computation.3 | async-start | bytes 4456448 | tf_op jit(solution)/shard_map/all_gather | solution.py:16
  9.6 493.5 %all-gather.8.cloned.1.call-start = ((), (), s32[]{:S(2)}) async-start(), calls=%async_computation.5 | async-start | bytes 2228224 | tf_op jit(solution)/shard_map/all_gather | solution.py:54
  362.7 5.6 copy-start
  362.7 98.3 %all-to-all-start = ((f32[128,16,256]{0,2,1:T(8,128)}), f32[128,16,256]{0,2,1:T(8,128)S(1)}, u32[]{:S(2)}, u32[]{:S(2)}) async-start(f32[128,16,256]{0,2,1:T(8,128)} %bitcast), calls=%async_computation.1 | async-start | bytes 4194304 | tf_op jit(solution)/shard_map/all_to_all | solution.py:53
  368.3 282.3 %reduce-scatter.2.cloned.1.call-start = ((), (), s32[]{:S(2)}) async-start(), calls=%async_computation.4 | async-start | bytes 2162688 | tf_op jit(solution)/shard_map/reduce_scatter | solution.py:50
Sparse Core Ops, SparseCore 0:
  10.7 67.3 all-gather.3
  81.2 138.4 all-gather.5
  362.8 140.2 all-gather.7
  506.3 144.2 reduce-scatter.1
where the time goes:
time: 659 us; the launch traced here: 658 us
  waiting for transfers between devices  391 us (59%)
  blocking collectives  221 us (34%)
  matrix products  18.6 us (3%)
  between operations  15.6 us (2%)
    all_gather x1, waiting for transfers between devices, body(): lax.all_gather(document_vectors, 'row', axis=1, tiled=True)  142 us
    reduce_scatter x1, waiting for transfers between devices, body(): lax.psum_scatter(query_terms, 'col', scatter_dimension=1, tiled=True)  141 us
    psum x1, blocking collectives, body(): lax.psum(jnp.sum(log_total - positive_score), 'row') / query_score_sum  86.1 us
    all_gather x1, waiting for transfers between devices, body(): full_queries = lax.all_gather(question_vectors, 'col', axis=1, tiled=True)  67.8 us
    psum x1, blocking collectives, body(): exp_total, positive_score = lax.psum((local_total, positive_local), 'col')  67.7 us
    pmax x1, blocking collectives, body(): topmost = lax.pmax(local_top, 'col')  67.4 us
    all_gather x1, waiting for transfers between devices, body(): lax.all_gather(normalized_likelihoods, 'row', axis=0, tiled=True)  40.3 us
  transfers between devices with their start and end apart: 5, of which 4 were waited for; matrix products, arithmetic and copies ran while one was open for 2% of the time, Pallas kernels for 0%

commit v1 on v0

v1 whole, which is shorter than its diff:
```python
import jax
import jax.numpy as jnp
from jax import lax
from jax.experimental import pallas as pl
from jax.experimental.pallas import tpu as pltpu
from jax.sharding import PartitionSpec as P

LIST = 4
NQ = 2048
INV = 20.0

K = 4
R = 64 // K
DP = 2
N_SEM = 47 * K + 24
ORDER = (
    1, 3, 4, 5, 6, 7, 8, 11, 12, 13, 15, 16, 17, 18, 19, 22, 23, 24, 26, 27, 28, 29, 30, 33, 34, 35, 37, 38,
    39, 40, 41, 44, 45, 46, 14, 25, 36, 0, 9, 20, 31, 42, 2, 10, 21, 32, 43, 0, 0, 3, 0, 0, 0, 14, 25, 36, 3,
    0, 14, 3, 3, 25, 0, 36, 14, 14, 3, 25, 25, 3, 36, 36, 14, 14, 4, 5, 25, 25, 36, 36, 15, 4, 16, 5, 26, 27,
    15, 4, 16, 37, 38, 26, 27, 15, 6, 37, 38, 26, 17, 37, 8, 7, 6, 28, 18, 19, 8, 7, 39, 17, 29, 30, 6, 18,
    19, 7, 28, 40, 41, 29, 39, 30, 17, 18, 40, 28, 41, 29, 39, 40, 9, 20, 10, 31, 11, 12, 42, 22, 23, 21, 32,
    13, 33, 34, 42, 24, 43, 2, 35, 1, 44, 45, 13, 2, 46, 24, 1, 1, 1, 1, 35, 13, 24, 46, 2, 1, 35, 46,
)

MESH = pl.DeviceIdType.MESH
F32 = jnp.float32
BF16 = jnp.bfloat16


def split2(a):
    hi = a.astype(BF16)
    return hi, (a - hi.astype(F32)).astype(BF16)


def split3(a):
    p1 = a.astype(BF16)
    r1 = a - p1.astype(F32)
    p2 = r1.astype(BF16)
    return p1, p2, (r1 - p2.astype(F32)).astype(BF16)


def dot_nt(a, b):
    return lax.dot_general(a, b, (((1,), (1,)), ((), ())), preferred_element_type=F32)


def dot_nn(a, b):
    return lax.dot_general(a, b, (((1,), (0,)), ((), ())), preferred_element_type=F32)


def dot_tn(a, b):
    return lax.dot_general(a, b, (((0,), (0,)), ((), ())), preferred_element_type=F32)


def kernel(
    q_ref, d_ref, pos_hbm, loss_ref, dq_ref, dd_ref,
    qbuf, qs, dbuf, ds_, dra, drb, sbuf, rl, rs, sg, ws, tcol, pack, tpack,
    stx, stz, tg, dqp, dqa, dqb, dxl, dxr, dz, dqt, dqo,
    dd, ddr, ddt, era, erb, ddz, lsum, lrecv, pos_ref, ssem, rsem, lsem,
):
    row = lax.axis_index("row")
    col = lax.axis_index("col")
    y, zh = lax.div(row, 2), lax.rem(row, 2)
    zl, core = lax.div(col, 8), lax.rem(col, 2)
    x = lax.rem(lax.div(col, 2), 4)
    z = zh * 4 + zl

    def dev(xx, yy, zz, cc):
        return (yy * 2 + lax.div(zz, 4), (lax.rem(zz, 4) * 4 + xx) * 2 + cc)

    def at_y(d):
        return dev(x, lax.rem(y + d + 8, 8), z, core)

    def at_z(d):
        return dev(x, y, lax.rem(z + d + 8, 8), core)

    def at_zl(d):
        return dev(x, y, zh * 4 + lax.rem(zl + d, 4), core)

    def at_x(d):
        return dev(lax.rem(x + d + 4, 4), y, z, core)

    def xi(xx):
        return (1 - lax.rem(xx, 2)) * 2 + lax.div(xx, 2)

    def xo(d):
        return xi(lax.rem(x + d + 4, 4))

    def blk(d):
        yy = lax.rem(y + d + 8, 8)
        b = lax.rem(yy, 2) * 4 + lax.div(yy, 2)
        return pl.ds(pl.multiple_of(b * R, R), R)

    def blk_b(d):
        yy = lax.rem(y + d + 8, 8)
        return lax.rem(yy, 2) * 4 + lax.div(yy, 2)

    other = dev(x, y, z, 1 - core)
    hx = 2 * lax.rem(y, 2) + 1 - lax.rem(x, 2)
    hy = 2 * zl + lax.div(x, 2)
    hz = zh * 4 + lax.div(y, 2)
    home = [dev(hx, hy, hz, core), dev(hx, hy, hz, 1 - core)]

    barrier = pltpu.get_barrier_semaphore()
    partners = [other, at_z(2), at_z(-2), at_z(4)] + [at_y(t) for t in range(1, 8)]
    partners += [at_zl(t) for t in (1, 2, 3)] + [at_x(t) for t in (1, 2, 3)] + home
    for p in partners:
        pl.semaphore_signal(barrier, inc=1, device_id=p, device_id_type=MESH)

    own_p = pl.ds(pl.multiple_of(core * 256, 256), 256)
    oth_p = pl.ds(pl.multiple_of((1 - core) * 256, 256), 256)
    get_pos = pltpu.make_async_copy(pos_hbm, pos_ref, lsem.at[0])
    get_pos.start()
    get_d = pltpu.make_async_copy(d_ref, dbuf.at[zh, own_p], lsem.at[1])
    get_d.start()
    pack[...] = jnp.zeros_like(pack)
    tpack[...] = jnp.zeros_like(tpack)
    pidx = (512 * (zl * 4 + x) + lax.broadcasted_iota(jnp.int32, (1, 512), 1)).astype(F32)
    lane = lax.broadcasted_iota(jnp.int32, (1, 128), 1)
    get_pos.wait()
    target = (LIST * (row * 128 + lane) + pos_ref[...]).astype(F32)
    tcol[...] = jnp.broadcast_to(target, (128, 128)).T
    get_d.wait()
    pl.semaphore_wait(barrier, len(partners))

    sends = []

    def send(src, dst, to):
        i = len(sends)
        cp = pltpu.make_async_remote_copy(
            src_ref=src, dst_ref=dst, send_sem=ssem.at[i], recv_sem=rsem.at[i],
            device_id=to, device_id_type=MESH,
        )
        cp.start()
        sends.append(cp)
        return cp

    def rows(start, size):
        return pl.ds(pl.multiple_of(start, size), size)

    half = 128 // DP

    def z_exchange(src, mid_a, mid_b, dst_a, dst_b, base):
        a = [send(src.at[i * half : (i + 1) * half], mid_a.at[i * half : (i + 1) * half], at_z(2)) for i in range(DP)]
        b = [send(src.at[128 + i * half : 128 + (i + 1) * half], mid_b.at[i * half : (i + 1) * half], at_z(-2))
             for i in range(DP)]
        last = []
        for i in range(DP):
            rw = slice(i * half, (i + 1) * half)
            yield
            a[i].wait_recv()
            last.append(send(mid_a.at[rw], dst_a.at[rows(base + i * half, half)], at_z(2)))
            yield
            b[i].wait_recv()
            last.append(send(mid_b.at[rw], dst_b.at[rows(base + 128 + i * half, half)], at_z(-2)))
        return last

    def documents():
        c = send(d_ref, dbuf.at[zh, own_p], other)
        below = dbuf.at[lax.div(lax.rem(z + 6, 8), 4)]
        above = dbuf.at[lax.div(lax.rem(z + 2, 8), 4)]
        last = yield from z_exchange(d_ref, dra, drb, below, above, core * 256)
        yield
        c.wait_recv()
        yield
        for cp in last:
            cp.wait_recv()
        e = send(dbuf.at[1 - zh, own_p], dbuf.at[1 - zh, own_p], other)
        yield
        e.wait_recv()
        for fh in range(2):
            for i, part in enumerate(split3(dbuf[fh])):
                ds_[i, fh] = part

    state = {}

    class Chunk:
        def __init__(self, k):
            self.k = k
            self.far = 1 if k % 2 == 0 else -1
            self.to_far, self.to_near = at_y(self.far), at_y(-self.far)
            self.pr, self.pq = k // 2, (k % 2) * 8 * R

        def queries(self):
            k = self.k
            cps = []
            for j in range(2):
                kc = core if j == 0 else 1 - core
                cps.append(send(
                    q_ref.at[rows(64 * kc + R * k, R)],
                    qbuf.at[k, lax.rem(x, 2) * 2 + lax.rem(y, 2), rows(lax.div(y, 2) * R, R),
                            pl.ds(pl.multiple_of(core * 128, 128), 128)],
                    home[j],
                ))
            yield
            for cp in cps:
                cp.wait_recv()
            mine = qbuf.at[k, xo(0), rows(zl * R, R)]
            cps = [send(mine, mine, at_zl(t)) for t in (1, 2, 3)]
            yield
            for cp in cps:
                cp.wait_recv()
            mine = qbuf.at[k, xo(0)]
            cr = send(mine, mine, at_x(1))
            cl = send(mine, mine, at_x(-1))
            yield
            cr.wait_recv()
            part = qbuf.at[k, xo(-1), 0 : 2 * R]
            rr = send(part, part, at_x(1))
            yield
            cl.wait_recv()
            part = qbuf.at[k, xo(1), 2 * R : 4 * R]
            rel = send(part, part, at_x(-1))
            yield
            rr.wait_recv()
            rel.wait_recv()
            for fh in range(2):
                whole = qbuf[k, 2 * fh : 2 * fh + 2].reshape(8 * R, 256)
                for i, part in enumerate(split3(whole)):
                    qs[self.pr, i, fh, self.pq : self.pq + 8 * R, :] = part
            yield

            def scores(i, carry):
                rw = pl.ds(pl.multiple_of(i * 128, 128), 128)
                qw = pl.ds(pl.multiple_of(self.pq + i * 128, 128), 128)
                acc = None
                for a, b in ((2, 0), (1, 1), (0, 2), (1, 0), (0, 1), (0, 0)):
                    for fh in range(2):
                        t = dot_nt(qs[self.pr, a, fh, qw, :], ds_[b, fh])
                        acc = t if acc is None else acc + t
                sbuf[k, rw, :] = acc
                return carry

            lax.fori_loop(0, 8 * R // 128, scores, 0)
            self.cf = send(sbuf.at[k, blk(4 * self.far)], rl.at[k, 0], self.to_far)
            self.cn = send(sbuf.at[k, blk(-3 * self.far)], rs.at[k, 0], self.to_near)

        def reduce_far(self):
            k = self.k
            for s in range(3):
                yield
                self.cf.wait_recv()
                rl[k, s] = rl[k, s] + sbuf[k, blk(self.far * (3 - s)), :]
                self.cf = send(rl.at[k, s], rl.at[k, s + 1], self.to_far)

        def reduce_near(self):
            k = self.k
            for s in range(2):
                yield
                self.cn.wait_recv()
                rs[k, s] = rs[k, s] + sbuf[k, blk(-self.far * (2 - s)), :]
                self.cn = send(rs.at[k, s], rs.at[k, s + 1], self.to_near)

        def join(self):
            k = self.k
            yield
            self.cf.wait_recv()
            self.cn.wait_recv()
            full = (sbuf[k, blk(0), :] + rs[k, 2] + rl[k, 3]) * INV
            sg[k, blk(0), :] = full
            mine = sg.at[k, blk(0)]
            self.af = send(mine, mine, self.to_far)
            self.an = send(mine, mine, self.to_near)
            tc = tcol[rows(64 * core + R * k, R), 0:1]
            top = jnp.max(full, axis=1, keepdims=True)
            total = jnp.sum(jnp.exp(full - top), axis=1, keepdims=True)
            hit = jnp.sum(jnp.where(tc == pidx, full, 0.0), axis=1, keepdims=True)
            ln = lax.broadcasted_iota(jnp.int32, (R, 128), 1)
            pack[k, 0:R, :] = jnp.where(ln == 0, top, jnp.where(ln == 1, total, jnp.where(ln == 2, hit, tc)))
            stx[k, x] = pack[k].T[0:8]
            cps = [send(stx.at[k, x], stx.at[k, x], at_x(t)) for t in (1, 2, 3)]
            yield
            for cp in cps:
                cp.wait_recv()
            stz[k, zl] = tile(*merge(stx[k]))
            cps = [send(stz.at[k, zl], stz.at[k, zl], at_zl(t)) for t in (1, 2, 3)]
            yield
            for cp in cps:
                cp.wait_recv()
            top, total, hit, tgt = merge(stz[k])
            mine = tg.at[k, blk_b(0)]
            tg[k, blk_b(0)] = tile(top + jnp.log(total), hit, tgt, tgt)
            self.g = [send(mine, mine, at_y(t)) for t in range(1, 8)]

        def gather_far(self):
            for s in range(3):
                yield
                self.af.wait_recv()
                part = sg.at[self.k, blk(-self.far * (1 + s))]
                self.af = send(part, part, self.to_far)

        def gather_near(self):
            for s in range(2):
                yield
                self.an.wait_recv()
                part = sg.at[self.k, blk(self.far * (1 + s))]
                self.an = send(part, part, self.to_near)

        def weights(self):
            k, pr, pq = self.k, self.pr, self.pq
            yield
            self.af.wait_recv()
            self.an.wait_recv()
            for cp in self.g:
                cp.wait_recv()
            for b in range(8):
                tpack[k, b : b + 1, :] = tg[k, b, 0:1, :]
                tpack[k, 8 + b : 9 + b, :] = tg[k, b, 2:3, :]
            tt = tpack[k].T
            for b in range(8):
                w = jnp.exp(sg[k, b * R : (b + 1) * R, :] - tt[0:R, b : b + 1])
                w = (w - jnp.where(tt[0:R, 8 + b : 9 + b] == pidx, 1.0, 0.0)) * INV
                w1, w2 = split2(w)
                ws[pr, 0, pq + b * R : pq + (b + 1) * R, :] = w1
                ws[pr, 1, pq + b * R : pq + (b + 1) * R, :] = w2
            if k == K - 1:
                yield
                self.dd_pair(1 - zh)
                state["e0"] = send(dd.at[1 - zh, oth_p], ddr.at[0], other)

            def some(i, carry):
                rw = pl.ds(pl.multiple_of(pq + i * 4 * R, 4 * R), 4 * R)
                for fh in range(2):
                    acc = dot_nn(ws[pr, 1, rw, :], ds_[0, fh])
                    acc = acc + dot_nn(ws[pr, 0, rw, :], ds_[1, fh])
                    dqp[k, 2 * fh + i] = acc + dot_nn(ws[pr, 0, rw, :], ds_[0, fh])
                return carry

            lax.fori_loop(0, 2, some, 0)
            self.ca = send(dqp.at[k, xo(2), 0 : 2 * R], dqa.at[k], at_x(1))
            self.cb = send(dqp.at[k, xo(2), 2 * R : 4 * R], dqb.at[k], at_x(-1))
            self.c1 = send(dqp.at[k, xo(1), 2 * R : 4 * R], dxl.at[k, 2 * R : 4 * R], at_x(1))
            self.c2 = send(dqp.at[k, xo(-1), 0 : 2 * R], dxr.at[k, 0 : 2 * R], at_x(-1))

        def dd_pair(self, fh):
            pr = self.pr
            acc = dot_tn(ws[pr, 1], qs[pr, 0, fh])
            acc = acc + dot_tn(ws[pr, 0], qs[pr, 1, fh])
            acc = acc + dot_tn(ws[pr, 0], qs[pr, 0, fh])
            if pr == 0:
                dd[fh] = acc
            else:
                dd[fh] = dd[fh] + acc

        def documents_term(self):
            yield
            if self.k == K - 1:
                self.dd_pair(zh)
                state["e1"] = send(dd.at[zh, oth_p], ddr.at[1], other)
            elif self.k % 2 == 1:
                self.dd_pair(0)
                self.dd_pair(1)

        def sum_right(self):
            k = self.k
            yield
            self.ca.wait_recv()
            dqa[k] = dqa[k] + dqp[k, xo(1), 0 : 2 * R, :]
            self.c3 = send(dqa.at[k], dxl.at[k, 0 : 2 * R], at_x(1))

        def sum_left(self):
            k = self.k
            yield
            self.cb.wait_recv()
            dqb[k] = dqb[k] + dqp[k, xo(-1), 2 * R : 4 * R, :]
            self.c4 = send(dqb.at[k], dxr.at[k, 2 * R : 4 * R], at_x(-1))

        def sum_join(self):
            k = self.k
            yield
            for cp in (self.c1, self.c2, self.c3, self.c4):
                cp.wait_recv()
            dqt[k] = dqp[k, xo(0)] + dxl[k] + dxr[k]
            cps = [send(dqt.at[k, rows(lax.rem(zl + t, 4) * R, R)], dz.at[k, t - 1], at_zl(t)) for t in (1, 2, 3)]
            yield
            for cp in cps:
                cp.wait_recv()
            mine = rows(zl * R, R)
            dqt[k, mine, :] = dqt[k, mine, :] + dz[k, 0] + dz[k, 1] + dz[k, 2]
            cps = []
            for j in range(2):
                kc = core if j == 0 else 1 - core
                cps.append(send(
                    dqt.at[k, mine, pl.ds(pl.multiple_of(kc * 128, 128), 128)],
                    dqo.at[rows(64 * core + R * k, R)],
                    home[j],
                ))
            yield
            for cp in cps:
                cp.wait_recv()

    sub = lax.broadcasted_iota(jnp.int32, (8, 128), 0)

    def merge(st):
        m = st[:, 0, :]
        top = jnp.max(m, axis=0, keepdims=True)
        total = jnp.sum(st[:, 1, :] * jnp.exp(m - top), axis=0, keepdims=True)
        hit = jnp.sum(st[:, 2, :], axis=0, keepdims=True)
        return top, total, hit, st[0, 3:4, :]

    def tile(a, b, c, d):
        return jnp.where(sub == 0, a, jnp.where(sub == 1, b, jnp.where(sub == 2, c, d)))

    def ending():
        yield
        state["e0"].wait_recv()
        ddt[...] = dd[1 - zh, own_p, :] + ddr[0]
        last = yield from z_exchange(ddt, era, erb, ddz, ddz, 0)
        yield
        state["e1"].wait_recv()
        for cp in last:
            cp.wait_recv()
        dd_ref[...] = dd[zh, own_p, :] + ddr[1] + ddz[...]

    def loss():
        yield
        part = jnp.zeros((8, 128), F32)
        for k in range(K):
            part = part + jnp.where(lane < R, tg[k, :, 0, :] - tg[k, :, 1, :], 0.0)
        lsum[0] = jnp.broadcast_to(jnp.sum(part, keepdims=True), (8, 128))
        cp = send(lsum.at[0], lrecv.at[0], other)
        yield
        cp.wait_recv()
        lsum[1] = lsum[0] + lrecv[0]
        cp = send(lsum.at[1], lrecv.at[1], at_z(4))
        yield
        cp.wait_recv()
        loss_ref[0, 0] = jnp.sum((lsum[1] + lrecv[1])[0:1, 0:1]) * (1.0 / NQ)

    threads = [documents(), ending(), loss()]
    for k in range(K):
        c = Chunk(k)
        threads += [
            c.queries(), c.reduce_far(), c.reduce_near(), c.join(), c.gather_far(), c.gather_near(),
            c.weights(), c.documents_term(), c.sum_right(), c.sum_left(), c.sum_join(),
        ]
    ended = 0
    for t in ORDER:
        if next(threads[t], True):
            ended += 1
    assert ended == len(threads)
    dq_ref[...] = dqo[...]
    for cp in sends:
        cp.wait_send()


def fused(question_vectors, document_vectors, positive):
    vmem = pl.BlockSpec(memory_space=pltpu.VMEM)
    hbm = pl.BlockSpec(memory_space=pl.ANY)
    smem = pl.BlockSpec(memory_space=pltpu.SMEM)
    v = pltpu.VMEM
    loss, dq, dd = pl.pallas_call(
        kernel,
        out_shape=(
            jax.ShapeDtypeStruct((1, 1), F32),
            jax.ShapeDtypeStruct((128, 128), F32),
            jax.ShapeDtypeStruct((256, 256), F32),
        ),
        in_specs=[hbm, hbm, hbm],
        out_specs=(smem, vmem, vmem),
        scratch_shapes=[
            v((K, 4, 4 * R, 256), F32),
            v((K // 2, 3, 2, 16 * R, 256), BF16),
            v((2, 512, 256), F32),
            v((3, 2, 512, 256), BF16),
            v((128, 256), F32),
            v((128, 256), F32),
            v((K, 8 * R, 512), F32),
            v((K, 4, R, 512), F32),
            v((K, 3, R, 512), F32),
            v((K, 8 * R, 512), F32),
            v((K // 2, 2, 16 * R, 512), BF16),
            v((128, 128), F32),
            v((K, 128, 128), F32),
            v((K, 128, 128), F32),
            v((K, 4, 8, 128), F32),
            v((K, 4, 8, 128), F32),
            v((K, 8, 8, 128), F32),
            v((K, 4, 4 * R, 256), F32),
            v((K, 2 * R, 256), F32),
            v((K, 2 * R, 256), F32),
            v((K, 4 * R, 256), F32),
            v((K, 4 * R, 256), F32),
            v((K, 3, R, 256), F32),
            v((K, 4 * R, 256), F32),
            v((128, 128), F32),
            v((2, 512, 256), F32),
            v((2, 256, 256), F32),
            v((256, 256), F32),
            v((128, 256), F32),
            v((128, 256), F32),
            v((256, 256), F32),
            v((2, 8, 128), F32),
            v((2, 8, 128), F32),
            v((1, 128), jnp.int32),
            pltpu.SemaphoreType.DMA((N_SEM,)),
            pltpu.SemaphoreType.DMA((N_SEM,)),
            pltpu.SemaphoreType.DMA((2,)),
        ],
        compiler_params=pltpu.CompilerParams(
            collective_id=0, has_side_effects=True, vmem_limit_bytes=40 * 1024 * 1024
        ),
        name="infonce",
    )(question_vectors, document_vectors, positive.reshape(1, 128))
    return loss.reshape(()), dq, dd


def solution(mesh):
    in_specs = (P("row", "col"), P("col", "row"), P("row"))
    out_specs = (P(), P("row", "col"), P("col", "row"))
    return jax.shard_map(fused, mesh=mesh, in_specs=in_specs, out_specs=out_specs, check_vma=False)
```

time: 659 us -> 122 us (0.19)
  the two profiles are of different devices: /device:TPU:48 before, /device:TPU:2 now
where the time goes in v1:
time: 122 us
  Pallas kernels  116 us (95%)
  local copies, waits for them, and re-layouts  3.77 us (3%)
  between operations  2.38 us (2%)
    pallas_call x1, Pallas kernels, fused(): pl.pallas_call(kernel, out_shape=(jax.ShapeDtypeStruct((1, 1), F32), jax....  116 us
    unnamed x8, local copies, waits for them, and re-layouts  3.77 us

profile of v1, /device:TPU:2, one launch (start us, length us, event | category | flops | bytes accessed | tf_op | source)
XLA Modules:
  0.0 122.0 jit_solution(4067214380347510939)
XLA Ops:
  0.6 0.0 copy-start.2
  0.6 0.6 copy-done.2
  1.3 0.0 copy-start
  1.3 0.9 copy-done
  2.2 0.0 copy-start.1
  2.2 0.8 copy-done.1
  3.1 115.8 %infonce.1 = (f32[1,1]{1,0:T(1,128)}, f32[128,128]{1,0:T(8,128)S(1)}, f32[256,256]{1,0:T(8,128)S(1)}) custom-call(f32[128,128]{1,0:T(8,128)S(1)} %copy-done.1, f32[256,256]{1,0:T(8,128)S(1)} %copy-done, s32[1,128]{1,0:T(1,128)S(1)} %bitcast.2), custom_call_target="tpu_custom_call" | custom-call | tf_op jit(solution)/shard_map/infonce/pallas_call | solution.py:451
  119.5 0.6 copy.10
  120.1 0.7 copy.11
Async XLA Ops:
  0.6 0.7 copy-start.2
  1.3 0.9 copy-start
  2.2 0.8 copy-start.1

commit v2 on v1

--- a/solution.py
+++ b/solution.py
@@ -445,7 +445,7 @@
 
 def fused(question_vectors, document_vectors, positive):
     vmem = pl.BlockSpec(memory_space=pltpu.VMEM)
-    hbm = pl.BlockSpec(memory_space=pl.ANY)
+    hbm = pl.BlockSpec(memory_space=pltpu.HBM)
     smem = pl.BlockSpec(memory_space=pltpu.SMEM)
     v = pltpu.VMEM
     loss, dq, dd = pl.pallas_call(

time: 122 us -> 122 us (level)
  no operation moved by 1% of the time
where the time goes in v2:
time: 122 us
  Pallas kernels  116 us (95%)
  local copies, waits for them, and re-layouts  3.77 us (3%)
  between operations  2.38 us (2%)
    pallas_call x1, Pallas kernels, fused(): pl.pallas_call(kernel, out_shape=(jax.ShapeDtypeStruct((1, 1), F32), jax....  116 us
    unnamed x8, local copies, waits for them, and re-layouts  3.77 us

profile of v2, /device:TPU:2, one launch (start us, length us, event | category | flops | bytes accessed | tf_op | source)
XLA Modules:
  0.0 122.0 jit_solution(4067214380347510939)
XLA Ops:
  0.6 0.0 copy-start.2
  0.6 0.6 copy-done.2
  1.3 0.0 copy-start
  1.3 0.9 copy-done
  2.2 0.0 copy-start.1
  2.2 0.8 copy-done.1
  3.1 115.8 %infonce.1 = (f32[1,1]{1,0:T(1,128)}, f32[128,128]{1,0:T(8,128)S(1)}, f32[256,256]{1,0:T(8,128)S(1)}) custom-call(f32[128,128]{1,0:T(8,128)S(1)} %copy-done.1, f32[256,256]{1,0:T(8,128)S(1)} %copy-done, s32[1,128]{1,0:T(1,128)S(1)} %bitcast.2), custom_call_target="tpu_custom_call" | custom-call | tf_op jit(solution)/shard_map/infonce/pallas_call | solution.py:451
  119.5 0.6 copy.10
  120.1 0.7 copy.11
Async XLA Ops:
  0.6 0.7 copy-start.2
  1.3 0.9 copy-start
  2.2 0.8 copy-start.1

commit v3 on v2

--- a/solution.py
+++ b/solution.py
@@ -12,14 +12,14 @@
 K = 4
 R = 64 // K
 DP = 2
-N_SEM = 47 * K + 24
+N_SEM = 56 * K + 24
 ORDER = (
-    1, 3, 4, 5, 6, 7, 8, 11, 12, 13, 15, 16, 17, 18, 19, 22, 23, 24, 26, 27, 28, 29, 30, 33, 34, 35, 37, 38,
-    39, 40, 41, 44, 45, 46, 14, 25, 36, 0, 9, 20, 31, 42, 2, 10, 21, 32, 43, 0, 0, 3, 0, 0, 0, 14, 25, 36, 3,
-    0, 14, 3, 3, 25, 0, 36, 14, 14, 3, 25, 25, 3, 36, 36, 14, 14, 4, 5, 25, 25, 36, 36, 15, 4, 16, 5, 26, 27,
-    15, 4, 16, 37, 38, 26, 27, 15, 6, 37, 38, 26, 17, 37, 8, 7, 6, 28, 18, 19, 8, 7, 39, 17, 29, 30, 6, 18,
-    19, 7, 28, 40, 41, 29, 39, 30, 17, 18, 40, 28, 41, 29, 39, 40, 9, 20, 10, 31, 11, 12, 42, 22, 23, 21, 32,
-    13, 33, 34, 42, 24, 43, 2, 35, 1, 44, 45, 13, 2, 46, 24, 1, 1, 1, 1, 35, 13, 24, 46, 2, 1, 35, 46,
+    0, 1, 3, 4, 5, 6, 7, 8, 11, 12, 13, 15, 16, 17, 18, 19, 22, 23, 24, 26, 27, 28, 29, 30, 33, 34, 35, 37,
+    38, 39, 40, 41, 44, 45, 46, 14, 25, 36, 2, 9, 10, 20, 21, 31, 32, 42, 43, 0, 0, 3, 0, 14, 0, 0, 25, 36,
+    3, 0, 14, 25, 3, 3, 36, 0, 14, 14, 25, 25, 3, 36, 3, 36, 14, 14, 25, 25, 5, 36, 36, 4, 16, 15, 27, 26,
+    38, 37, 6, 17, 28, 7, 8, 6, 18, 19, 39, 17, 30, 29, 28, 40, 41, 39, 9, 20, 31, 10, 11, 12, 21, 42, 22,
+    23, 32, 42, 33, 34, 43, 13, 2, 24, 1, 44, 45, 35, 2, 13, 46, 24, 1, 1, 1, 1, 13, 35, 46, 24, 2, 1, 35,
+    46,
 )
 
 MESH = pl.DeviceIdType.MESH
@@ -54,7 +54,7 @@
 def kernel(
     q_ref, d_ref, pos_hbm, loss_ref, dq_ref, dd_ref,
     qbuf, qs, dbuf, ds_, dra, drb, sbuf, rl, rs, sg, ws, tcol, pack, tpack,
-    stx, stz, tg, dqp, dqa, dqb, dxl, dxr, dz, dqt, dqo,
+    stx, tg, dqp, dqa, dqb, dxl, dxr, dz, dqt, dqo,
     dd, ddr, ddt, era, erb, ddz, lsum, lrecv, pos_ref, ssem, rsem, lsem,
 ):
     row = lax.axis_index("row")
@@ -79,6 +79,9 @@
     def at_x(d):
         return dev(lax.rem(x + d + 4, 4), y, z, core)
 
+    def at_grid(t):
+        return dev(lax.rem(x + t % 4, 4), y, zh * 4 + lax.rem(zl + t // 4, 4), core)
+
     def xi(xx):
         return (1 - lax.rem(xx, 2)) * 2 + lax.div(xx, 2)
 
@@ -102,7 +105,7 @@
 
     barrier = pltpu.get_barrier_semaphore()
     partners = [other, at_z(2), at_z(-2), at_z(4)] + [at_y(t) for t in range(1, 8)]
-    partners += [at_zl(t) for t in (1, 2, 3)] + [at_x(t) for t in (1, 2, 3)] + home
+    partners += [at_grid(t) for t in range(1, 16)] + home
     for p in partners:
         pl.semaphore_signal(barrier, inc=1, device_id=p, device_id_type=MESH)
 
@@ -177,7 +180,6 @@
         def __init__(self, k):
             self.k = k
             self.far = 1 if k % 2 == 0 else -1
-            self.to_far, self.to_near = at_y(self.far), at_y(-self.far)
             self.pr, self.pq = k // 2, (k % 2) * 8 * R
 
         def queries(self):
@@ -231,76 +233,76 @@
                 return carry
 
             lax.fori_loop(0, 8 * R // 128, scores, 0)
-            self.cf = send(sbuf.at[k, blk(4 * self.far)], rl.at[k, 0], self.to_far)
-            self.cn = send(sbuf.at[k, blk(-3 * self.far)], rs.at[k, 0], self.to_near)
+            f = self.far
+            self.m1 = send(sbuf.at[k, blk(4 * f)], rl.at[k, 0], at_y(2 * f))
+            self.m2 = send(sbuf.at[k, blk(3 * f)], rl.at[k, 1], at_y(f))
+            self.n1 = send(sbuf.at[k, blk(-3 * f)], rs.at[k, 0], at_y(-f))
+            self.m4 = send(sbuf.at[k, blk(f)], rl.at[k, 3], at_y(f))
+            self.n3 = send(sbuf.at[k, blk(-f)], rs.at[k, 2], at_y(-f))
 
         def reduce_far(self):
-            k = self.k
-            for s in range(3):
-                yield
-                self.cf.wait_recv()
-                rl[k, s] = rl[k, s] + sbuf[k, blk(self.far * (3 - s)), :]
-                self.cf = send(rl.at[k, s], rl.at[k, s + 1], self.to_far)
+            k, f = self.k, self.far
+            yield
+            self.m1.wait_recv()
+            self.m2.wait_recv()
+            rl[k, 0] = rl[k, 0] + rl[k, 1] + sbuf[k, blk(2 * f), :]
+            self.m3 = send(rl.at[k, 0], rl.at[k, 2], at_y(2 * f))
 
         def reduce_near(self):
-            k = self.k
-            for s in range(2):
-                yield
-                self.cn.wait_recv()
-                rs[k, s] = rs[k, s] + sbuf[k, blk(-self.far * (2 - s)), :]
-                self.cn = send(rs.at[k, s], rs.at[k, s + 1], self.to_near)
+            k, f = self.k, self.far
+            yield
+            self.n1.wait_recv()
+            rs[k, 0] = rs[k, 0] + sbuf[k, blk(-2 * f), :]
+            self.n2 = send(rs.at[k, 0], rs.at[k, 1], at_y(-2 * f))
 
         def join(self):
-            k = self.k
-            yield
-            self.cf.wait_recv()
-            self.cn.wait_recv()
-            full = (sbuf[k, blk(0), :] + rs[k, 2] + rl[k, 3]) * INV
+            k, f = self.k, self.far
+            yield
+            for cp in (self.m3, self.m4, self.n2, self.n3):
+                cp.wait_recv()
+            full = (sbuf[k, blk(0), :] + rs[k, 1] + rs[k, 2] + rl[k, 2] + rl[k, 3]) * INV
             sg[k, blk(0), :] = full
             mine = sg.at[k, blk(0)]
-            self.af = send(mine, mine, self.to_far)
-            self.an = send(mine, mine, self.to_near)
+            self.a2 = send(mine, mine, at_y(2 * f))
+            self.b2 = send(mine, mine, at_y(-2 * f))
+            self.a1 = send(mine, mine, at_y(f))
+            self.b1 = send(mine, mine, at_y(-f))
             tc = tcol[rows(64 * core + R * k, R), 0:1]
             top = jnp.max(full, axis=1, keepdims=True)
             total = jnp.sum(jnp.exp(full - top), axis=1, keepdims=True)
             hit = jnp.sum(jnp.where(tc == pidx, full, 0.0), axis=1, keepdims=True)
             ln = lax.broadcasted_iota(jnp.int32, (R, 128), 1)
             pack[k, 0:R, :] = jnp.where(ln == 0, top, jnp.where(ln == 1, total, jnp.where(ln == 2, hit, tc)))
-            stx[k, x] = pack[k].T[0:8]
-            cps = [send(stx.at[k, x], stx.at[k, x], at_x(t)) for t in (1, 2, 3)]
+            stx[k, zl * 4 + x] = pack[k].T[0:8]
+            mine = stx.at[k, zl * 4 + x]
+            cps = [send(mine, mine, at_grid(t)) for t in range(1, 16)]
             yield
             for cp in cps:
                 cp.wait_recv()
-            stz[k, zl] = tile(*merge(stx[k]))
-            cps = [send(stz.at[k, zl], stz.at[k, zl], at_zl(t)) for t in (1, 2, 3)]
-            yield
-            for cp in cps:
-                cp.wait_recv()
-            top, total, hit, tgt = merge(stz[k])
+            top, total, hit, tgt = merge(stx[k])
             mine = tg.at[k, blk_b(0)]
             tg[k, blk_b(0)] = tile(top + jnp.log(total), hit, tgt, tgt)
             self.g = [send(mine, mine, at_y(t)) for t in range(1, 8)]
 
         def gather_far(self):
-            for s in range(3):
-                yield
-                self.af.wait_recv()
-                part = sg.at[self.k, blk(-self.far * (1 + s))]
-                self.af = send(part, part, self.to_far)
+            f = self.far
+            yield
+            self.a2.wait_recv()
+            part = sg.at[self.k, blk(-2 * f)]
+            self.a4 = send(part, part, at_y(2 * f))
+            self.a3 = send(part, part, at_y(f))
 
         def gather_near(self):
-            for s in range(2):
-                yield
-                self.an.wait_recv()
-                part = sg.at[self.k, blk(self.far * (1 + s))]
-                self.an = send(part, part, self.to_near)
+            f = self.far
+            yield
+            self.b2.wait_recv()
+            part = sg.at[self.k, blk(2 * f)]
+            self.b3 = send(part, part, at_y(-f))
 
         def weights(self):
             k, pr, pq = self.k, self.pr, self.pq
             yield
-            self.af.wait_recv()
-            self.an.wait_recv()
-            for cp in self.g:
+            for cp in [self.a1, self.a3, self.a4, self.b1, self.b3] + self.g:
                 cp.wait_recv()
             for b in range(8):
                 tpack[k, b : b + 1, :] = tg[k, b, 0:1, :]
@@ -472,8 +474,7 @@
             v((128, 128), F32),
             v((K, 128, 128), F32),
             v((K, 128, 128), F32),
-            v((K, 4, 8, 128), F32),
-            v((K, 4, 8, 128), F32),
+            v((K, 16, 8, 128), F32),
             v((K, 8, 8, 128), F32),
             v((K, 4, 4 * R, 256), F32),
             v((K, 2 * R, 256), F32),

time: 122 us -> 122 us (level)
  the two profiles are of different devices: /device:TPU:2 before, /device:TPU:61 now
where the time goes in v3:
time: 122 us; the launch traced here: 121 us
  Pallas kernels  115 us (94%)
  local copies, waits for them, and re-layouts  3.77 us (3%)
  between operations  2.38 us (2%)
    pallas_call x1, Pallas kernels, fused(): pl.pallas_call(kernel, out_shape=(jax.ShapeDtypeStruct((1, 1), F32), jax....  115 us
    unnamed x8, local copies, waits for them, and re-layouts  3.77 us

profile of v3, /device:TPU:61, one launch (start us, length us, event | category | flops | bytes accessed | tf_op | source)
XLA Modules:
  0.0 121.4 jit_solution(6608863524018059425)
XLA Ops:
  0.6 0.0 copy-start.2
  0.6 0.6 copy-done.2
  1.3 0.0 copy-start
  1.3 0.9 copy-done
  2.2 0.0 copy-start.1
  2.2 0.8 copy-done.1
  3.1 115.2 %infonce.1 = (f32[1,1]{1,0:T(1,128)}, f32[128,128]{1,0:T(8,128)S(1)}, f32[256,256]{1,0:T(8,128)S(1)}) custom-call(f32[128,128]{1,0:T(8,128)S(1)} %copy-done.1, f32[256,256]{1,0:T(8,128)S(1)} %copy-done, s32[1,128]{1,0:T(1,128)S(1)} %bitcast.2), custom_call_target="tpu_custom_call" | custom-call | tf_op jit(solution)/shard_map/infonce/pallas_call | solution.py:453
  118.9 0.6 copy.10
  119.6 0.7 copy.11
Async XLA Ops:
  0.6 0.7 copy-start.2
  1.3 0.9 copy-start
  2.2 0.8 copy-start.1

commit v4 on v3

--- a/solution.py
+++ b/solution.py
@@ -47,13 +47,9 @@
     return lax.dot_general(a, b, (((1,), (0,)), ((), ())), preferred_element_type=F32)
 
 
-def dot_tn(a, b):
-    return lax.dot_general(a, b, (((0,), (0,)), ((), ())), preferred_element_type=F32)
-
-
 def kernel(
     q_ref, d_ref, pos_hbm, loss_ref, dq_ref, dd_ref,
-    qbuf, qs, dbuf, ds_, dra, drb, sbuf, rl, rs, sg, ws, tcol, pack, tpack,
+    qbuf, qs, dbuf, ds_, dra, drb, sbuf, rl, rs, sg, ws, wts, tcol, pack, tpack,
     stx, tg, dqp, dqa, dqb, dxl, dxr, dz, dqt, dqo,
     dd, ddr, ddt, era, erb, ddz, lsum, lrecv, pos_ref, ssem, rsem, lsem,
 ):
@@ -308,26 +304,24 @@
                 tpack[k, b : b + 1, :] = tg[k, b, 0:1, :]
                 tpack[k, 8 + b : 9 + b, :] = tg[k, b, 2:3, :]
             tt = tpack[k].T
-            for b in range(8):
-                w = jnp.exp(sg[k, b * R : (b + 1) * R, :] - tt[0:R, b : b + 1])
-                w = (w - jnp.where(tt[0:R, 8 + b : 9 + b] == pidx, 1.0, 0.0)) * INV
-                w1, w2 = split2(w)
-                ws[pr, 0, pq + b * R : pq + (b + 1) * R, :] = w1
-                ws[pr, 1, pq + b * R : pq + (b + 1) * R, :] = w2
+            top = jnp.concatenate([tt[0:R, b : b + 1] for b in range(8)], axis=0)
+            tgt = jnp.concatenate([tt[0:R, 8 + b : 9 + b] for b in range(8)], axis=0)
+            w = (jnp.exp(sg[k] - top) - jnp.where(tgt == pidx, 1.0, 0.0)) * INV
+            for i, part in enumerate(split2(w)):
+                ws[pr, i, pq : pq + 8 * R, :] = part
+            for i, part in enumerate(split2(w.T)):
+                wts[pr, i, :, pq : pq + 8 * R] = part
             if k == K - 1:
                 yield
                 self.dd_pair(1 - zh)
                 state["e0"] = send(dd.at[1 - zh, oth_p], ddr.at[0], other)
 
-            def some(i, carry):
-                rw = pl.ds(pl.multiple_of(pq + i * 4 * R, 4 * R), 4 * R)
-                for fh in range(2):
-                    acc = dot_nn(ws[pr, 1, rw, :], ds_[0, fh])
-                    acc = acc + dot_nn(ws[pr, 0, rw, :], ds_[1, fh])
-                    dqp[k, 2 * fh + i] = acc + dot_nn(ws[pr, 0, rw, :], ds_[0, fh])
-                return carry
-
-            lax.fori_loop(0, 2, some, 0)
+            rw = slice(pq, pq + 8 * R)
+            for fh in range(2):
+                acc = dot_nn(ws[pr, 1, rw, :], ds_[0, fh]) + dot_nn(ws[pr, 0, rw, :], ds_[1, fh])
+                acc = acc + dot_nn(ws[pr, 0, rw, :], ds_[0, fh])
+                dqp[k, 2 * fh] = acc[0 : 4 * R]
+                dqp[k, 2 * fh + 1] = acc[4 * R : 8 * R]
             self.ca = send(dqp.at[k, xo(2), 0 : 2 * R], dqa.at[k], at_x(1))
             self.cb = send(dqp.at[k, xo(2), 2 * R : 4 * R], dqb.at[k], at_x(-1))
             self.c1 = send(dqp.at[k, xo(1), 2 * R : 4 * R], dxl.at[k, 2 * R : 4 * R], at_x(1))
@@ -335,9 +329,9 @@
 
         def dd_pair(self, fh):
             pr = self.pr
-            acc = dot_tn(ws[pr, 1], qs[pr, 0, fh])
-            acc = acc + dot_tn(ws[pr, 0], qs[pr, 1, fh])
-            acc = acc + dot_tn(ws[pr, 0], qs[pr, 0, fh])
+            acc = dot_nn(wts[pr, 1], qs[pr, 0, fh])
+            acc = acc + dot_nn(wts[pr, 0], qs[pr, 1, fh])
+            acc = acc + dot_nn(wts[pr, 0], qs[pr, 0, fh])
             if pr == 0:
                 dd[fh] = acc
             else:
@@ -471,6 +465,7 @@
             v((K, 3, R, 512), F32),
             v((K, 8 * R, 512), F32),
             v((K // 2, 2, 16 * R, 512), BF16),
+            v((K // 2, 2, 512, 16 * R), BF16),
             v((128, 128), F32),
             v((K, 128, 128), F32),
             v((K, 128, 128), F32),

time: 122 us -> 121 us (level)
  no operation moved by 1% of the time
where the time goes in v4:
time: 121 us
  Pallas kernels  115 us (95%)
  local copies, waits for them, and re-layouts  3.77 us (3%)
  between operations  2.38 us (2%)
    pallas_call x1, Pallas kernels, fused(): pl.pallas_call(kernel, out_shape=(jax.ShapeDtypeStruct((1, 1), F32), jax....  115 us
    unnamed x8, local copies, waits for them, and re-layouts  3.77 us

profile of v4, /device:TPU:61, one launch (start us, length us, event | category | flops | bytes accessed | tf_op | source)
XLA Modules:
  0.0 120.9 jit_solution(16874641156147692462)
XLA Ops:
  0.6 0.0 copy-start.2
  0.6 0.6 copy-done.2
  1.3 0.0 copy-start
  1.3 0.9 copy-done
  2.2 0.0 copy-start.1
  2.2 0.8 copy-done.1
  3.1 114.8 %infonce.1 = (f32[1,1]{1,0:T(1,128)}, f32[128,128]{1,0:T(8,128)S(1)}, f32[256,256]{1,0:T(8,128)S(1)}) custom-call(f32[128,128]{1,0:T(8,128)S(1)} %copy-done.1, f32[256,256]{1,0:T(8,128)S(1)} %copy-done, s32[1,128]{1,0:T(1,128)S(1)} %bitcast.2), custom_call_target="tpu_custom_call" | custom-call | tf_op jit(solution)/shard_map/infonce/pallas_call | solution.py:447
  118.5 0.6 copy.10
  119.1 0.7 copy.11
Async XLA Ops:
  0.6 0.7 copy-start.2
  1.3 0.9 copy-start
  2.2 0.8 copy-start.1

commit v5 on v4

--- a/solution.py
+++ b/solution.py
@@ -9,17 +9,14 @@
 NQ = 2048
 INV = 20.0
 
-K = 4
+K = 2
 R = 64 // K
 DP = 2
 N_SEM = 56 * K + 24
 ORDER = (
-    0, 1, 3, 4, 5, 6, 7, 8, 11, 12, 13, 15, 16, 17, 18, 19, 22, 23, 24, 26, 27, 28, 29, 30, 33, 34, 35, 37,
-    38, 39, 40, 41, 44, 45, 46, 14, 25, 36, 2, 9, 10, 20, 21, 31, 32, 42, 43, 0, 0, 3, 0, 14, 0, 0, 25, 36,
-    3, 0, 14, 25, 3, 3, 36, 0, 14, 14, 25, 25, 3, 36, 3, 36, 14, 14, 25, 25, 5, 36, 36, 4, 16, 15, 27, 26,
-    38, 37, 6, 17, 28, 7, 8, 6, 18, 19, 39, 17, 30, 29, 28, 40, 41, 39, 9, 20, 31, 10, 11, 12, 21, 42, 22,
-    23, 32, 42, 33, 34, 43, 13, 2, 24, 1, 44, 45, 35, 2, 13, 46, 24, 1, 1, 1, 1, 13, 35, 46, 24, 2, 1, 35,
-    46,
+    1, 3, 4, 5, 6, 7, 8, 11, 12, 13, 15, 16, 17, 18, 19, 22, 23, 24, 14, 0, 9, 20, 2, 10, 21, 0, 0, 3, 0, 0,
+    0, 14, 3, 0, 14, 0, 3, 3, 14, 14, 3, 3, 14, 14, 5, 4, 16, 15, 6, 17, 6, 7, 8, 17, 18, 19, 9, 20, 10, 20,
+    21, 11, 12, 2, 1, 22, 23, 2, 13, 24, 1, 1, 1, 1, 13, 2, 1, 24, 13, 24,
 )
 
 MESH = pl.DeviceIdType.MESH

time: 121 us -> 121 us (level)
  the two profiles are of different devices: /device:TPU:61 before, /device:TPU:35 now
where the time goes in v5:
time: 121 us
  Pallas kernels  115 us (95%)
  local copies, waits for them, and re-layouts  3.77 us (3%)
  between operations  2.38 us (2%)
    pallas_call x1, Pallas kernels, fused(): pl.pallas_call(kernel, out_shape=(jax.ShapeDtypeStruct((1, 1), F32), jax....  115 us
    unnamed x8, local copies, waits for them, and re-layouts  3.77 us

profile of v5, /device:TPU:35, one launch (start us, length us, event | category | flops | bytes accessed | tf_op | source)
XLA Modules:
  0.0 121.2 jit_solution(834830020130457934)
XLA Ops:
  0.6 0.0 copy-start.2
  0.6 0.6 copy-done.2
  1.3 0.0 copy-start
  1.3 0.9 copy-done
  2.2 0.0 copy-start.1
  2.2 0.8 copy-done.1
  3.1 115.0 %infonce.1 = (f32[1,1]{1,0:T(1,128)}, f32[128,128]{1,0:T(8,128)S(1)}, f32[256,256]{1,0:T(8,128)S(1)}) custom-call(f32[128,128]{1,0:T(8,128)S(1)} %copy-done.1, f32[256,256]{1,0:T(8,128)S(1)} %copy-done, s32[1,128]{1,0:T(1,128)S(1)} %bitcast.2), custom_call_target="tpu_custom_call" | custom-call | tf_op jit(solution)/shard_map/infonce/pallas_call | solution.py:444
  118.7 0.6 copy.10
  119.4 0.7 copy.11
Async XLA Ops:
  0.6 0.7 copy-start.2
  1.3 0.9 copy-start
  2.2 0.8 copy-start.1

commit v6 on v4

--- a/solution.py
+++ b/solution.py
@@ -15,11 +15,10 @@
 N_SEM = 56 * K + 24
 ORDER = (
     0, 1, 3, 4, 5, 6, 7, 8, 11, 12, 13, 15, 16, 17, 18, 19, 22, 23, 24, 26, 27, 28, 29, 30, 33, 34, 35, 37,
-    38, 39, 40, 41, 44, 45, 46, 14, 25, 36, 2, 9, 10, 20, 21, 31, 32, 42, 43, 0, 0, 3, 0, 14, 0, 0, 25, 36,
-    3, 0, 14, 25, 3, 3, 36, 0, 14, 14, 25, 25, 3, 36, 3, 36, 14, 14, 25, 25, 5, 36, 36, 4, 16, 15, 27, 26,
-    38, 37, 6, 17, 28, 7, 8, 6, 18, 19, 39, 17, 30, 29, 28, 40, 41, 39, 9, 20, 31, 10, 11, 12, 21, 42, 22,
-    23, 32, 42, 33, 34, 43, 13, 2, 24, 1, 44, 45, 35, 2, 13, 46, 24, 1, 1, 1, 1, 13, 35, 46, 24, 2, 1, 35,
-    46,
+    38, 39, 40, 41, 44, 45, 46, 14, 25, 36, 2, 9, 10, 20, 21, 31, 32, 42, 43, 0, 0, 3, 0, 0, 0, 14, 25, 36,
+    3, 0, 14, 3, 3, 25, 0, 36, 14, 3, 14, 25, 3, 25, 36, 14, 36, 14, 5, 4, 25, 25, 16, 36, 36, 15, 27, 6, 26,
+    38, 37, 17, 17, 7, 8, 28, 18, 19, 39, 17, 39, 30, 29, 41, 40, 39, 9, 20, 11, 12, 31, 22, 10, 21, 23, 42,
+    13, 33, 34, 32, 42, 24, 13, 35, 43, 44, 45, 1, 2, 24, 46, 13, 2, 35, 1, 1, 1, 24, 1, 46, 35, 2, 1, 46,
 )
 
 MESH = pl.DeviceIdType.MESH
@@ -171,6 +170,8 @@
                 ds_[i, fh] = part
 
     state = {}
+    packed = set()
+    totals = {}
 
     class Chunk:
         def __init__(self, k):
@@ -268,17 +269,23 @@
             total = jnp.sum(jnp.exp(full - top), axis=1, keepdims=True)
             hit = jnp.sum(jnp.where(tc == pidx, full, 0.0), axis=1, keepdims=True)
             ln = lax.broadcasted_iota(jnp.int32, (R, 128), 1)
-            pack[k, 0:R, :] = jnp.where(ln == 0, top, jnp.where(ln == 1, total, jnp.where(ln == 2, hit, tc)))
-            stx[k, zl * 4 + x] = pack[k].T[0:8]
-            mine = stx.at[k, zl * 4 + x]
+            pr, half = self.pr, (k % 2) * R
+            pack[pr, half : half + R, :] = jnp.where(ln == 0, top, jnp.where(ln == 1, total, jnp.where(ln == 2, hit, tc)))
+            if k % 2 == 0:
+                packed.add(pr)
+                return
+            yield
+            assert pr in packed
+            stx[pr, zl * 4 + x] = pack[pr].T[0:8]
+            mine = stx.at[pr, zl * 4 + x]
             cps = [send(mine, mine, at_grid(t)) for t in range(1, 16)]
             yield
             for cp in cps:
                 cp.wait_recv()
-            top, total, hit, tgt = merge(stx[k])
-            mine = tg.at[k, blk_b(0)]
-            tg[k, blk_b(0)] = tile(top + jnp.log(total), hit, tgt, tgt)
-            self.g = [send(mine, mine, at_y(t)) for t in range(1, 8)]
+            top, total, hit, tgt = merge(stx[pr])
+            mine = tg.at[pr, blk_b(0)]
+            tg[pr, blk_b(0)] = tile(top + jnp.log(total), hit, tgt, tgt)
+            totals[pr] = [send(mine, mine, at_y(t)) for t in range(1, 8)]
 
         def gather_far(self):
             f = self.far
@@ -298,14 +305,16 @@
         def weights(self):
             k, pr, pq = self.k, self.pr, self.pq
             yield
-            for cp in [self.a1, self.a3, self.a4, self.b1, self.b3] + self.g:
-                cp.wait_recv()
+            for cp in [self.a1, self.a3, self.a4, self.b1, self.b3] + totals[pr]:
+                cp.wait_recv()
+            totals[pr] = []
+            half = (k % 2) * R
             for b in range(8):
-                tpack[k, b : b + 1, :] = tg[k, b, 0:1, :]
-                tpack[k, 8 + b : 9 + b, :] = tg[k, b, 2:3, :]
+                tpack[k, b : b + 1, :] = tg[pr, b, 0:1, :]
+                tpack[k, 8 + b : 9 + b, :] = tg[pr, b, 2:3, :]
             tt = tpack[k].T
-            top = jnp.concatenate([tt[0:R, b : b + 1] for b in range(8)], axis=0)
-            tgt = jnp.concatenate([tt[0:R, 8 + b : 9 + b] for b in range(8)], axis=0)
+            top = jnp.concatenate([tt[half : half + R, b : b + 1] for b in range(8)], axis=0)
+            tgt = jnp.concatenate([tt[half : half + R, 8 + b : 9 + b] for b in range(8)], axis=0)
             w = (jnp.exp(sg[k] - top) - jnp.where(tgt == pidx, 1.0, 0.0)) * INV
             for i, part in enumerate(split2(w)):
                 ws[pr, i, pq : pq + 8 * R, :] = part
@@ -410,8 +419,8 @@
     def loss():
         yield
         part = jnp.zeros((8, 128), F32)
-        for k in range(K):
-            part = part + jnp.where(lane < R, tg[k, :, 0, :] - tg[k, :, 1, :], 0.0)
+        for pr in range(K // 2):
+            part = part + jnp.where(lane < 2 * R, tg[pr, :, 0, :] - tg[pr, :, 1, :], 0.0)
         lsum[0] = jnp.broadcast_to(jnp.sum(part, keepdims=True), (8, 128))
         cp = send(lsum.at[0], lrecv.at[0], other)
         yield
@@ -467,10 +476,10 @@
             v((K // 2, 2, 16 * R, 512), BF16),
             v((K // 2, 2, 512, 16 * R), BF16),
             v((128, 128), F32),
+            v((K // 2, 128, 128), F32),
             v((K, 128, 128), F32),
-            v((K, 128, 128), F32),
-            v((K, 16, 8, 128), F32),
-            v((K, 8, 8, 128), F32),
+            v((K // 2, 16, 8, 128), F32),
+            v((K // 2, 8, 8, 128), F32),
             v((K, 4, 4 * R, 256), F32),
             v((K, 2 * R, 256), F32),
             v((K, 2 * R, 256), F32),

time: 121 us -> 122 us (level)
  no operation moved by 1% of the time
where the time goes in v6:
time: 122 us
  Pallas kernels  116 us (95%)
  local copies, waits for them, and re-layouts  3.77 us (3%)
  between operations  2.38 us (2%)
    pallas_call x1, Pallas kernels, fused(): pl.pallas_call(kernel, out_shape=(jax.ShapeDtypeStruct((1, 1), F32), jax....  116 us
    unnamed x8, local copies, waits for them, and re-layouts  3.77 us

profile of v6, /device:TPU:61, one launch (start us, length us, event | category | flops | bytes accessed | tf_op | source)
XLA Modules:
  0.0 121.8 jit_solution(2354862589061634009)
XLA Ops:
  0.6 0.0 copy-start.2
  0.6 0.6 copy-done.2
  1.3 0.0 copy-start
  1.3 0.9 copy-done
  2.2 0.0 copy-start.1
  2.2 0.8 copy-done.1
  3.1 115.7 %infonce.1 = (f32[1,1]{1,0:T(1,128)}, f32[128,128]{1,0:T(8,128)S(1)}, f32[256,256]{1,0:T(8,128)S(1)}) custom-call(f32[128,128]{1,0:T(8,128)S(1)} %copy-done.1, f32[256,256]{1,0:T(8,128)S(1)} %copy-done, s32[1,128]{1,0:T(1,128)S(1)} %bitcast.2), custom_call_target="tpu_custom_call" | custom-call | tf_op jit(solution)/shard_map/infonce/pallas_call | solution.py:456
  119.4 0.6 copy.10
  120.0 0.7 copy.11
Async XLA Ops:
  0.6 0.7 copy-start.2
  1.3 0.9 copy-start
  2.2 0.8 copy-start.1

commit v7 on v5

--- a/solution.py
+++ b/solution.py
@@ -14,9 +14,9 @@
 DP = 2
 N_SEM = 56 * K + 24
 ORDER = (
-    1, 3, 4, 5, 6, 7, 8, 11, 12, 13, 15, 16, 17, 18, 19, 22, 23, 24, 14, 0, 9, 20, 2, 10, 21, 0, 0, 3, 0, 0,
-    0, 14, 3, 0, 14, 0, 3, 3, 14, 14, 3, 3, 14, 14, 5, 4, 16, 15, 6, 17, 6, 7, 8, 17, 18, 19, 9, 20, 10, 20,
-    21, 11, 12, 2, 1, 22, 23, 2, 13, 24, 1, 1, 1, 1, 13, 2, 1, 24, 13, 24,
+    1, 3, 4, 6, 8, 5, 11, 7, 12, 13, 15, 16, 18, 19, 22, 23, 24, 14, 17, 0, 2, 9, 20, 10, 21, 0, 0, 3, 0, 0,
+    0, 14, 3, 0, 14, 3, 3, 0, 14, 14, 3, 3, 14, 14, 5, 4, 16, 15, 6, 17, 6, 7, 8, 18, 17, 19, 9, 20, 10, 20,
+    21, 11, 12, 2, 1, 22, 23, 13, 24, 1, 1, 1, 1, 13, 2, 24, 1, 2, 24, 13,
 )
 
 MESH = pl.DeviceIdType.MESH

time: 121 us -> 119 us (0.983)
  the two profiles are of different devices: /device:TPU:35 before, /device:TPU:61 now
where the time goes in v7:
time: 119 us
  Pallas kernels  113 us (95%)
  local copies, waits for them, and re-layouts  3.77 us (3%)
  between operations  2.38 us (2%)
    pallas_call x1, Pallas kernels, fused(): pl.pallas_call(kernel, out_shape=(jax.ShapeDtypeStruct((1, 1), F32), jax....  113 us
    unnamed x8, local copies, waits for them, and re-layouts  3.77 us

profile of v7, /device:TPU:61, one launch (start us, length us, event | category | flops | bytes accessed | tf_op | source)
XLA Modules:
  0.0 118.7 jit_solution(5961205856783018149)
XLA Ops:
  0.6 0.0 copy-start.2
  0.6 0.6 copy-done.2
  1.3 0.0 copy-start
  1.3 0.9 copy-done
  2.2 0.0 copy-start.1
  2.2 0.8 copy-done.1
  3.1 112.6 %infonce.1 = (f32[1,1]{1,0:T(1,128)}, f32[128,128]{1,0:T(8,128)S(1)}, f32[256,256]{1,0:T(8,128)S(1)}) custom-call(f32[128,128]{1,0:T(8,128)S(1)} %copy-done.1, f32[256,256]{1,0:T(8,128)S(1)} %copy-done, s32[1,128]{1,0:T(1,128)S(1)} %bitcast.2), custom_call_target="tpu_custom_call" | custom-call | tf_op jit(solution)/shard_map/infonce/pallas_call | solution.py:444
  116.3 0.6 copy.10
  116.9 0.7 copy.11
Async XLA Ops:
  0.6 0.7 copy-start.2
  1.3 0.9 copy-start
  2.2 0.8 copy-start.1

commit v8 on v7

--- a/solution.py
+++ b/solution.py
@@ -14,9 +14,9 @@
 DP = 2
 N_SEM = 56 * K + 24
 ORDER = (
-    1, 3, 4, 6, 8, 5, 11, 7, 12, 13, 15, 16, 18, 19, 22, 23, 24, 14, 17, 0, 2, 9, 20, 10, 21, 0, 0, 3, 0, 0,
-    0, 14, 3, 0, 14, 3, 3, 0, 14, 14, 3, 3, 14, 14, 5, 4, 16, 15, 6, 17, 6, 7, 8, 18, 17, 19, 9, 20, 10, 20,
-    21, 11, 12, 2, 1, 22, 23, 13, 24, 1, 1, 1, 1, 13, 2, 24, 1, 2, 24, 13,
+    3, 4, 1, 6, 8, 5, 11, 7, 12, 13, 15, 16, 18, 19, 0, 23, 24, 14, 17, 20, 2, 9, 10, 21, 0, 22, 0, 3, 0, 0,
+    0, 14, 3, 0, 3, 14, 3, 0, 14, 14, 3, 3, 14, 14, 5, 4, 16, 15, 6, 17, 8, 6, 7, 18, 17, 19, 9, 20, 10, 20,
+    21, 11, 12, 1, 2, 22, 23, 13, 24, 1, 1, 13, 1, 1, 2, 24, 1, 2, 24, 13,
 )
 
 MESH = pl.DeviceIdType.MESH

time: 119 us -> 120 us (level)
  the two profiles are of different devices: /device:TPU:61 before, /device:TPU:49 now
where the time goes in v8:
time: 120 us; the launch traced here: 119 us
  Pallas kernels  113 us (94%)
  local copies, waits for them, and re-layouts  3.77 us (3%)
  between operations  2.38 us (2%)
    pallas_call x1, Pallas kernels, fused(): pl.pallas_call(kernel, out_shape=(jax.ShapeDtypeStruct((1, 1), F32), jax....  113 us
    unnamed x8, local copies, waits for them, and re-layouts  3.77 us

profile of v8, /device:TPU:49, one launch (start us, length us, event | category | flops | bytes accessed | tf_op | source)
XLA Modules:
  0.0 119.4 jit_solution(5256232309749495761)
XLA Ops:
  0.6 0.0 copy-start.2
  0.6 0.6 copy-done.2
  1.3 0.0 copy-start
  1.3 0.9 copy-done
  2.2 0.0 copy-start.1
  2.2 0.8 copy-done.1
  3.1 113.2 %infonce.1 = (f32[1,1]{1,0:T(1,128)}, f32[128,128]{1,0:T(8,128)S(1)}, f32[256,256]{1,0:T(8,128)S(1)}) custom-call(f32[128,128]{1,0:T(8,128)S(1)} %copy-done.1, f32[256,256]{1,0:T(8,128)S(1)} %copy-done, s32[1,128]{1,0:T(1,128)S(1)} %bitcast.2), custom_call_target="tpu_custom_call" | custom-call | tf_op jit(solution)/shard_map/infonce/pallas_call | solution.py:444
  116.9 0.6 copy.10
  117.6 0.7 copy.11
Async XLA Ops:
  0.6 0.7 copy-start.2
  1.3 0.9 copy-start
  2.2 0.8 copy-start.1
